TPU v7x, 512 devices: a whole 4x8x8 slice. The times are simulated.
512 devices in a mesh: scen: 2 (over core), wide: 64 (over y, z), blk: 4 (over x).
Axes of the slice: x: 4, y: 8, z: 8, core: 2. Of those that a mesh axis runs over, the one named last changes fastest.
Arguments:
- weather: bfloat16 [8192, 128], P('scen'), parts along dimension 0, may hold values from -6 to 6
- response: bfloat16 [8192, 64, 128], P('wide', 'blk'), may hold values from -0.0625 to 0.0625
- coupling: bfloat16 [64, 2, 128, 128], P('wide'), may hold values from -0.375 to 0.375
- sources: int32 [64, 2], replicated, may hold values from 0 to 63
- delays: int32 [64, 2], replicated, may hold values from 1 to 16, as said below
Outputs:
- temps: bfloat16 [16384, 4096], P(('scen', 'wide'), 'blk'), parts along dimension 0
There are 2 independent parts, one for each index of `scen`. A program takes and returns all parts, laid end to end along the dimension named above; an argument that names none is the same for every part. Nothing has to cross between parts.
Inputs may be any that keep to these rules, and one draw needn't show every extreme that they name: `delays`: delay of each edge in steps; some edge has delay 16.
All inputs are finite; a program needn't handle non-finite values.
Results may differ from a plain program's by a relative error of at most 0.0085.
Values may be sent and summed in bfloat16 or wider, within the bound.
A program may use at most 64 MiB of HBM per device.

v0:
```python
import math

import jax
import jax.numpy as jnp
from jax import lax
from jax.sharding import PartitionSpec as P

LAGS = 64
BS = 128
DEG = 2
STEPS_DEV = 16


def passed_along(block, axis, distance):
    devices = range(lax.axis_size(axis))
    route = [(i - distance, i) for i in devices if i - distance in devices]
    return lax.ppermute(block, axis, route)


def transport(extended, out_rows, coupling, sources, delays):
    margin = extended.shape[0] - out_rows
    local_part = extended[margin:].astype(jnp.float32)
    blocked = extended.reshape(extended.shape[0], -1, BS)
    weight_piece = lax.all_gather(coupling, "wide", axis=0, tiled=True)
    block_count = weight_piece.shape[0]
    chosen = sources.reshape(-1)
    lag_values = delays.reshape(-1)
    upstream = jnp.transpose(jnp.take(blocked, chosen, axis=1), (1, 0, 2))

    def cut_series(single, lag_value):
        return lax.dynamic_slice_in_dim(single, margin - lag_value, out_rows, 0)

    moved = jax.vmap(cut_series)(upstream, lag_values)
    moved = moved.reshape(block_count, DEG, out_rows, BS)
    summed = jnp.einsum("kerb,kebc->rkc", moved, weight_piece, preferred_element_type=jnp.float32)
    carried = summed.reshape(out_rows, block_count * BS)
    return local_part + carried


def make_terms(padded_drive, response_part, lag_base, wide_count, blk_count):
    node_local = response_part.shape[0]
    lag_local = response_part.shape[1]
    total_rows = wide_count * blk_count * STEPS_DEV
    block_rows = math.gcd(total_rows, 512)
    window_rows = block_rows + lag_local - 1

    def one_block(first_row):
        start = first_row + (LAGS - 1) - lag_base - (lag_local - 1)
        window = lax.dynamic_slice_in_dim(padded_drive, start, window_rows, 0)
        spread = jnp.einsum(
            "ic,nlc->iln", window, response_part, preferred_element_type=jnp.float32
        )
        summed = spread[lag_local - 1 : lag_local - 1 + block_rows, 0]
        for lag_index in range(1, lag_local):
            summed = (
                summed
                + spread[
                    lag_local - 1 - lag_index : lag_local - 1 - lag_index + block_rows, lag_index
                ]
            )
        return summed

    starts = jnp.arange(total_rows // block_rows, dtype=jnp.int32) * block_rows
    demand = lax.map(one_block, starts).reshape(wide_count, blk_count, STEPS_DEV, node_local)
    ordered = jnp.transpose(demand, (1, 0, 2, 3)).reshape(total_rows, node_local)

    def term_rows(first_row, row_count):
        return ordered

    return term_rows


def body(weather, response, coupling, sources, delays):
    wide_count = lax.axis_size("wide")
    blk_count = lax.axis_size("blk")
    node_local = response.shape[0]
    padded_drive = jnp.pad(weather, ((LAGS - 1, 0), (0, 0)))
    slice_rows = wide_count * STEPS_DEV
    lag_local = response.shape[1]
    term_rows = make_terms(
        padded_drive, response, lax.axis_index("blk") * lag_local, wide_count, blk_count
    )
    own_rows = lax.psum_scatter(
        term_rows(jnp.int32(0), slice_rows * lax.axis_size("blk")),
        "blk",
        scatter_dimension=0,
        tiled=True,
    )
    load_rows = own_rows.astype(jnp.bfloat16)
    load = lax.all_to_all(load_rows, "wide", split_axis=0, concat_axis=1, tiled=True)

    def extend_series(series):
        previous = passed_along(series, ("wide", "blk"), 1)
        return jnp.concatenate([previous, series], axis=0)

    first = transport(extend_series(load), STEPS_DEV, coupling, sources, delays).astype(
        jnp.bfloat16
    )
    second = transport(extend_series(first), STEPS_DEV, coupling, sources, delays)
    result = second.astype(jnp.bfloat16).reshape(STEPS_DEV, wide_count, node_local)
    result = lax.all_to_all(result, "wide", split_axis=1, concat_axis=1, tiled=True)
    result = result.reshape(STEPS_DEV, blk_count, wide_count // blk_count, 1, node_local)
    result = lax.all_to_all(result, "blk", split_axis=1, concat_axis=3, tiled=True)
    result = result.reshape(STEPS_DEV, wide_count // blk_count, blk_count, node_local)
    return jnp.transpose(result, (3, 1, 2, 0)).reshape(node_local, -1)


def solution(mesh):
    placed = (P("scen", None), P("wide", "blk", None), P("wide", None, None, None), P(), P())
    return jax.shard_map(
        body, mesh=mesh, in_specs=placed, out_specs=P(("scen", "wide"), "blk"), check_vma=False
    )
```

profile of v0, /device:TPU:6, one launch (start us, length us, event | category | flops | bytes accessed | tf_op | source)
XLA Modules:
  0.0 193.9 jit_solution(11687144297532464092)
XLA Ops:
  7.4 1.2 copy.44
  8.6 1.5 pad.5
  10.1 23.4 %while.14 = (s32[]{:T(128)}, f32[8,512,128]{2,1,0:T(8,128)}, s32[8]{0:T(128)S(1)}, s32[]{:T(128)}, bf16[4159,128]{1,0:T(8,128)(2,1)S(1)}, /*index=5*/bf16[128,16...) while((s32[]{:T(128)}, f32[8,512,128]{2,1,0:T(8,128)}, ...), condition=%wide.region_1.2_spmd, body=%wide.region_0.1_spmd.sunk | while | flops 277282816 | bytes 9433795 | solution.py:64
  11.2 0.7 convolution_bitcast_fusion.3
  11.9 1.1 fusion.25
  14.1 0.7 convolution_bitcast_fusion.3
  14.9 1.1 fusion.25
  17.8 1.1 fusion.25
  20.7 1.1 fusion.25
  23.6 1.1 fusion.25
  26.6 1.1 fusion.25
  29.5 1.1 fusion.25
  32.4 1.1 fusion.25
  33.5 3.1 %copy.45 = f32[4,64,16,128]{3,2,1,0:T(8,128)} copy(f32[4,64,16,128]{3,2,0,1:T(8,128)} %bitcast.5) | data formatting | bytes 4194304 | tf_op jit(solution)/shard_map/transpose | solution.py:65
  37.5 37.0 %reduce-scatter.2.cloned.1.call-done = f32[1024,128]{1,0:T(8,128)} async-done(((f32[4096,128]{1,0:T(8,128)}), f32[1024,128]{1,0:T(8,128)}) %reduce-scatter.2.cloned.1.call-update) | async-done | bytes 524304 | tf_op jit(solution)/shard_map/reduce_scatter | solution.py:83
  74.6 1.8 convert_element_type.25
  76.3 13.3 %all-to-all-start = ((bf16[64,16,128]{2,1,0:T(8,128)(2,1)}), bf16[64,16,128]{2,1,0:T(8,128)(2,1)S(1)}, u32[]{:S(2)}, u32[]{:S(2)}) async-start(bf16[64,16,128]{2,1,0:T(8,128)(2,1)} %bitcast.7), calls=%async_computation.1 | async-start | bytes 524288 | tf_op jit(solution)/shard_map/all_to_all | solution.py:90
  89.7 15.0 %all-to-all-done = bf16[64,16,128]{2,1,0:T(8,128)(2,1)S(1)} async-done(((bf16[64,16,128]{2,1,0:T(8,128)(2,1)}), bf16[64,16,128]{2,1,0:T(8,128)(2,1)S(1)}, u32[]{:S(2)}, u32[]{:S(2)}) %all-to-all-start) | async-done | bytes 262176 | tf_op jit(solution)/shard_map/all_to_all | solution.py:90
  104.7 4.5 %collective-permute-start = (bf16[16,8192]{1,0:T(8,128)(2,1)S(1)}, bf16[16,8192]{1,0:T(8,128)(2,1)S(1)}, u32[]{:S(2)}, u32[]{:S(2)}) collective-permute-start(bf16[16,8192]{1,0:T(8,128)(2,1)S(1)} %copy_bitcast_fusion.1), channel_id=1, source_target_pairs={{0,1},{1,2},{2,3},{3,4},{4,5},{5,6},{6,7},{7,8},{8,9},{9,10},{10,1... | collective-permute-start | bytes 786440 | tf_op jit(solution)/shard_map/ppermute | solution.py:17
  109.7 10.0 %collective-permute-done = bf16[16,8192]{1,0:T(8,128)(2,1)S(1)} collective-permute-done((bf16[16,8192]{1,0:T(8,128)(2,1)S(1)}, bf16[16,8192]{1,0:T(8,128)(2,1)S(1)}, u32[]{:S(2)}, u32[]{:S(2)}) %collective-permute-start) | collective-permute-done | bytes 262176 | tf_op jit(solution)/shard_map/ppermute | solution.py:17
  119.8 0.8 gather_fusion.2
  121.2 2.8 %gather_fusion = bf16[128,16,128]{2,0,1:T(8,128)(2,1)S(1)} fusion(bf16[128,32,128]{2,0,1:T(8,128)(2,1)S(1)} %copy.51, s32[128]{0:T(128)S(1)} %or_bitcast_fusion), kind=kCustom, calls=%fused_computation.2 | custom fusion | bytes 1050112 | tf_op jit(solution)/shard_map/vmap()/gather | solution.py:31
  124.0 11.6 %all-gather.2.cloned.1.call-done = bf16[64,2,128,128]{3,2,1,0:T(8,128)(2,1)} async-done(((bf16[1,2,128,128]{3,2,1,0:T(8,128)(2,1)}), bf16[64,2,128,128]{3,2,1,0:T(8,128)(2,1)}) %all-gather.2.cloned.1.call-update) | async-done | bytes 4194320 | tf_op jit(solution)/shard_map/all_gather | solution.py:24
  135.6 3.0 %fusion.10 = f32[64,16,128,1]{2,1,3,0:T(8,128)S(1)} fusion(bf16[64,2,128,128]{3,2,1,0:T(8,128)(2,1)} %all-gather.2.cloned.1.call-done, bf16[64,2,16,128]{3,1,0,2:T(2,128)(2,1)S(1)} %bitcast.98), kind=kOutput, calls=%fused_computation.38 | convolution fusion | flops 67108864 | bytes 5242880 | tf_op jit(solution)/shard_map/kerb,kebc->rkc/dot_general | solution.py:35
  138.7 1.9 collective-permute-start.1
  140.6 6.3 %collective-permute-done.1 = bf16[16,8192]{1,0:T(8,128)(2,1)S(1)} collective-permute-done((bf16[16,8192]{1,0:T(8,128)(2,1)S(1)}, bf16[16,8192]{1,0:T(8,128)(2,1)S(1)}, u32[]{:S(2)}, u32[]{:S(2)}) %collective-permute-start.1) | collective-permute-done | bytes 262176 | tf_op jit(solution)/shard_map/ppermute | solution.py:17
  147.0 0.8 gather_fusion.3
  148.4 2.8 %gather_fusion.1 = bf16[128,16,128]{2,0,1:T(8,128)(2,1)S(1)} fusion(bf16[128,32,128]{2,0,1:T(8,128)(2,1)S(1)} %copy.55, s32[128]{0:T(128)S(1)} %or_bitcast_fusion), kind=kCustom, calls=%fused_computation.3 | custom fusion | bytes 1050112 | tf_op jit(solution)/shard_map/vmap()/gather | solution.py:31
  151.2 3.1 %fusion.6 = bf16[16,64,128]{2,0,1:T(8,128)(2,1)S(1)} fusion(bf16[64,2,128,128]{3,2,1,0:T(8,128)(2,1)} %all-gather.2.cloned.1.call-done, bf16[64,2,16,128]{3,1,0,2:T(2,128)(2,1)S(1)} %bitcast.99, f32[64,16,128,1]{2,1,3,0:T(8,128)S(1)} %fusion.10, bf16[64,16,128]{2,1,0:T(8,128)(2,1)S(1)} %all-to-all-done), kind=kOutput, calls=%fused_computation.27 | convolution fusion | flops 67895296 | bytes 5767168 | tf_op jit(solution)/shard_map/kerb,kebc->rkc/dot_general | solution.py:35
  154.3 21.4 %all_to_all.39 = bf16[16,64,128]{2,0,1:T(8,128)(2,1)S(1)} all-to-all(bf16[16,64,128]{2,0,1:T(8,128)(2,1)S(1)} %fusion.6), channel_id=1, replica_groups=mesh['scen'=2,'wide'=64,'blk'=4] {'wide'}, dimensions={1} | all-to-all | bytes 524288 | tf_op jit(solution)/shard_map/all_to_all | solution.py:101
  175.7 9.9 %all_to_all.40 = bf16[16,4,16,1,128]{4,0,2,3,1:T(8,128)(2,1)S(1)} all-to-all(bf16[16,4,16,1,128]{4,0,2,3,1:T(8,128)(2,1)S(1)} %bitcast.100), channel_id=1, replica_groups=mesh['scen'=2,'wide'=64,'blk'=4] {'blk'}, dimensions={1} | all-to-all | bytes 524288 | tf_op jit(solution)/shard_map/all_to_all | solution.py:103
  185.6 0.9 copy.59
  (45 shorter events, 11.7 us)
Async XLA Ops:
  7.4 67.2 %reduce-scatter.2.cloned.1.call-start = ((), (), s32[]{:S(2)}) async-start(), calls=%async_computation.4 | async-start | bytes 2621440 | tf_op jit(solution)/shard_map/reduce_scatter | solution.py:83
  36.6 0.7 copy-start
  36.6 53.0 %copy-start.1 = (s32[64,2]{0,1:T(2,128)S(1)}, s32[64,2]{0,1:T(2,128)}, u32[]{:S(2)}) copy-start(s32[64,2]{0,1:T(2,128)} %param.13) | copy-start | bytes 1540
  36.6 98.9 %all-gather.2.cloned.1.call-start = ((), (), s32[]{:S(2)}) async-start(), calls=%async_computation.5 | async-start | bytes 4259840 | tf_op jit(solution)/shard_map/all_gather | solution.py:24
  76.3 28.3 %all-to-all-start = ((bf16[64,16,128]{2,1,0:T(8,128)(2,1)}), bf16[64,16,128]{2,1,0:T(8,128)(2,1)S(1)}, u32[]{:S(2)}, u32[]{:S(2)}) async-start(bf16[64,16,128]{2,1,0:T(8,128)(2,1)} %bitcast.7), calls=%async_computation.1 | async-start | bytes 524288 | tf_op jit(solution)/shard_map/all_to_all | solution.py:90
  104.7 15.0 %collective-permute-start = (bf16[16,8192]{1,0:T(8,128)(2,1)S(1)}, bf16[16,8192]{1,0:T(8,128)(2,1)S(1)}, u32[]{:S(2)}, u32[]{:S(2)}) collective-permute-start(bf16[16,8192]{1,0:T(8,128)(2,1)S(1)} %copy_bitcast_fusion.1), channel_id=1, source_target_pairs={{0,1},{1,2},{2,3},{3,4},{4,5},{5,6},{6,7},{7,8},{8,9},{9,10},{10,1... | collective-permute-start | bytes 786440 | tf_op jit(solution)/shard_map/ppermute | solution.py:17
  138.7 8.3 %collective-permute-start.1 = (bf16[16,8192]{1,0:T(8,128)(2,1)S(1)}, bf16[16,8192]{1,0:T(8,128)(2,1)S(1)}, u32[]{:S(2)}, u32[]{:S(2)}) collective-permute-start(bf16[16,8192]{1,0:T(8,128)(2,1)S(1)} %fusion.7), channel_id=1, source_target_pairs={{0,1},{1,2},{2,3},{3,4},{4,5},{5,6},{6,7},{7,8},{8,9},{9,10},{10,1... | collective-permute-start | bytes 786440 | tf_op jit(solution)/shard_map/ppermute | solution.py:17
Sparse Core Ops, SparseCore 0:
  36.8 37.7 reduce-scatter.1
Sparse Core Ops, SparseCore 1:
  40.1 95.4 all-gather.1
where the time goes:
time: 195 us; the launch traced here: 194 us
  waiting for transfers between devices  80.5 us (41%)
  blocking collectives  31.3 us (16%)
  local copies, waits for them, and re-layouts  19.8 us (10%)
  starting transfers between devices  19.7 us (10%)
  between operations  15 us (8%)
  matrix products  12 us (6%)
  other arithmetic  11 us (6%)
  loops' own time  4.55 us (2%)
    reduce_scatter x1, waiting for transfers between devices, body(): lax.psum_scatter(term_rows(jnp.int32(0), slice_rows * lax.axis_size('blk'...  37 us
    all_to_all x1, blocking collectives, body(): lax.all_to_all(result, 'wide', split_axis=1, concat_axis=1, tiled=True)  21.4 us
    ppermute x2, waiting for transfers between devices, passed_along(): return lax.ppermute(block, axis, route)  16.3 us
    all_to_all x1, waiting for transfers between devices, body(): lax.all_to_all(load_rows, 'wide', split_axis=0, concat_axis=1, tiled=True)  15 us
    all_to_all x1, starting transfers between devices, body(): lax.all_to_all(load_rows, 'wide', split_axis=0, concat_axis=1, tiled=True)  13.3 us
    all_gather x1, waiting for transfers between devices, transport(): weight_piece = lax.all_gather(coupling, 'wide', axis=0, tiled=True)  11.6 us
    all_to_all x1, blocking collectives, body(): lax.all_to_all(result, 'blk', split_axis=1, concat_axis=3, tiled=True)  9.88 us
    dynamic_update_slice x8, other arithmetic, make_terms(): lax.map(one_block, starts)  8.63 us
  transfers between devices with their start and end apart: 5, of which 5 were waited for; matrix products, arithmetic and copies ran while one was open for 3% of the time, Pallas kernels for 0%

commit v1 on v0

v1 whole, which is shorter than its diff:
```python
import functools

import jax
import jax.numpy as jnp
from jax import lax
from jax.experimental import pallas as pl
from jax.experimental.pallas import tpu as pltpu
from jax.sharding import PartitionSpec as P

MESH = pl.DeviceIdType.MESH
CH = 128
LAGS = 64
BS = 128
HALO = 16
RING = 8
BLOCKS = 64
HALF = 32
ROWS = 32
QUARTER = HALF * ROWS
EXT = QUARTER + 2 * HALO
LROWS = ROWS + 2 * HALO
FROWS = ROWS + HALO
PIECE = 4
PARTS = 4
GROUP = 16
XROWS = EXT + LAGS - GROUP
WPRE = 96
TILE = 352


def drain(ref, sem):
    pltpu.make_async_copy(ref, ref, sem).wait()


def kernel(
    weather,
    resp,
    coupling,
    sources,
    delays,
    out,
    wraw,
    w32,
    xbuf,
    rbuf,
    acc,
    lext,
    lbuf,
    l32,
    fbuf,
    f32b,
    sbuf,
    cown,
    cmir,
    loc_sem,
    own_sem,
    self_sem,
    a_send,
    a_recv,
    am_send,
    am_recv,
    c1_send,
    c1_recv,
    c2_send,
    c2_recv,
    cm_send,
    cm_recv,
    b_send,
    b_recv,
    bm_send,
    bm_recv,
    f_send,
    f_recv,
    e_send,
    e_recv,
):
    s = lax.axis_index("scen")
    w = lax.axis_index("wide")
    x = lax.axis_index("blk")
    y, z = w // RING, w % RING
    first_core = s == 0
    u = jnp.where(first_core, z, y)
    v = jnp.where(first_core, y, z)
    right, left = (x + 1) % PARTS, (x + PARTS - 1) % PARTS
    far = (x + 2) % PARTS

    def wide_of(uu, vv):
        return jnp.where(first_core, vv * RING + uu, uu * RING + vv)

    def remote(src, dst, send, recv, core, wide, blk):
        return pltpu.make_async_remote_copy(
            src_ref=src,
            dst_ref=dst,
            send_sem=send,
            recv_sem=recv,
            device_id=(core, wide, blk),
            device_id_type=MESH,
        )

    sister = (1 - s, w, x)
    core_t = w // HALF
    slot = w % HALF
    own_target = core_t == s

    lead = pl.multiple_of(jnp.maximum(x * QUARTER - WPRE, 0), 32)
    here = pl.multiple_of(x * QUARTER, QUARTER)
    main_copy = pltpu.make_async_copy(
        weather.at[pl.ds(here, QUARTER)], wraw.at[pl.ds(WPRE, QUARTER)], loc_sem.at[0]
    )
    lead_copy = pltpu.make_async_copy(
        weather.at[pl.ds(lead, WPRE)], wraw.at[pl.ds(0, WPRE)], loc_sem.at[1]
    )
    resp_copy = pltpu.make_async_copy(resp, rbuf.at[pl.ds(4 * x, 4)], own_sem.at[0])
    coup_copy = pltpu.make_async_copy(coupling.at[0, s], cown.at[v * RING + u], own_sem.at[1])
    main_copy.start()
    lead_copy.start()
    resp_copy.start()
    coup_copy.start()

    barrier = pltpu.get_barrier_semaphore()

    def greet(core, wide, blk):
        pl.semaphore_signal(barrier, inc=1, device_id=(core, wide, blk), device_id_type=MESH)

    greet(s, w, right)
    greet(s, w, left)
    greet(*sister)

    @pl.loop(1, RING)
    def _(step):
        greet(s, wide_of((u + step) % RING, v), x)

    greet(s, wide_of(u, (v + 1) % RING), x)
    greet(s, wide_of(u, (v + RING - 1) % RING), x)

    @pl.loop(1, HALF)
    def _(step):
        greet(core_t, HALF * s + (slot + step) % HALF, x)

    @pl.when(jnp.logical_not(own_target))
    def _():
        greet(core_t, HALF * s + slot, x)

    pl.semaphore_wait(barrier, 3 + RING - 1 + 2 + HALF - 1 + jnp.where(own_target, 0, 1))

    def a_copy(index, src, piece, blk):
        return remote(src, rbuf.at[piece], a_send.at[index], a_recv.at[index], s, w, blk)

    p0, p1 = 2 * s, 2 * s + 1
    a_copies = [
        a_copy(0, resp.at[p0], 4 * x + p0, right),
        a_copy(1, resp.at[p1], 4 * x + p1, left),
        a_copy(2, resp.at[p1], 4 * x + p1, right),
        a_copy(3, resp.at[p0], 4 * x + p0, left),
    ]
    for copy in a_copies:
        copy.start()

    own_row = v * RING + u

    @pl.loop(1, RING)
    def _(step):
        remote(
            coupling.at[0, s],
            cown.at[own_row],
            c1_send,
            c1_recv,
            s,
            wide_of((u + step) % RING, v),
            x,
        ).start()

    main_copy.wait()
    lead_copy.wait()

    @pl.when(x == 0)
    def _():
        wraw[pl.ds(0, WPRE), :] = jnp.zeros((WPRE, CH), jnp.bfloat16)

    w32[...] = wraw[...].astype(jnp.float32)
    for lag in range(GROUP):
        xbuf[:, lag * CH : (lag + 1) * CH] = w32[GROUP - lag : GROUP - lag + XROWS, :].astype(
            jnp.bfloat16
        )

    def add_group(group, first):
        base = (LAGS - GROUP) - GROUP * group

        @pl.loop(0, EXT // TILE)
        def _(tile):
            row = pl.multiple_of(tile * TILE, 16)
            start = pl.multiple_of(base + row, 16)
            total = None
            for piece in range(4):
                term = lax.dot_general(
                    xbuf[pl.ds(start, TILE), piece * PIECE * CH : (piece + 1) * PIECE * CH],
                    rbuf[4 * group + piece],
                    (((1,), (1,)), ((), ())),
                    preferred_element_type=jnp.float32,
                )
                total = term if total is None else total + term
            if not first:
                total = total + acc[pl.ds(row, TILE), :]
            acc[pl.ds(row, TILE), :] = total

    resp_copy.wait()
    add_group(x, True)

    def mirror_piece(piece, group_sem):
        remote(
            rbuf.at[piece], rbuf.at[piece], am_send, am_recv.at[group_sem], *sister
        ).start()

    a_copies[0].wait_recv()
    fwd_right = a_copy(4, rbuf.at[4 * left + p0], 4 * left + p0, right)
    fwd_right.start()
    mirror_piece(4 * left + p0, 0)
    a_copies[1].wait_recv()
    fwd_left = a_copy(5, rbuf.at[4 * right + p1], 4 * right + p1, left)
    fwd_left.start()
    mirror_piece(4 * right + p1, 1)

    coup_copy.wait()
    drain(cown.at[pl.ds(0, RING - 1)], c1_recv)

    def needed(row, half):
        return jnp.where(first_core, row // 4 == 1, half == 0)

    def c_chunk(row, half):
        return cown.at[pl.ds(row * RING + 4 * half, 4)]

    def c_mirror(row, half):
        @pl.when(needed(row, half))
        def _():
            remote(
                c_chunk(row, half),
                cmir.at[pl.ds(row * RING + 4 * half, 4)],
                cm_send,
                cm_recv,
                *sister,
            ).start()

    def c_step(way, step, half):
        if way == 0:
            row, to = (v + RING - step + 1) % RING, (v + 1) % RING
        else:
            row, to = (v + step - 1) % RING, (v + RING - 1) % RING
        index = (way * 4 + step - 1) * 2 + half
        return remote(
            c_chunk(row, half),
            c_chunk(row, half),
            c2_send,
            c2_recv.at[index],
            s,
            wide_of(u, to),
            x,
        )

    def c_start(step):
        for half in range(2):
            for way in range(2):
                if step < 4 or half == way:
                    c_step(way, step, half).start()

    def c_arrive(step):
        for half in range(2):
            for way in range(2):
                if step < 4 or half == way:
                    c_step(way, step, half).wait_recv()
                    if step < 3 or (step == 3 and half == way):
                        c_step(way, step + 1, half).start()
                    row = (v + RING - step) % RING if way == 0 else (v + step) % RING
                    c_mirror(row, half)

    c_start(1)
    c_mirror(v, 0)
    c_mirror(v, 1)

    a_copies[2].wait_recv()
    mirror_piece(4 * left + p1, 0)
    a_copies[3].wait_recv()
    mirror_piece(4 * right + p0, 1)
    c_arrive(1)
    fwd_right.wait_recv()
    mirror_piece(4 * far + p0, 2)
    fwd_left.wait_recv()
    mirror_piece(4 * far + p1, 2)
    drain(rbuf.at[pl.ds(0, 2)], am_recv.at[0])
    add_group(left, False)
    drain(rbuf.at[pl.ds(0, 2)], am_recv.at[1])
    add_group(right, False)
    drain(rbuf.at[pl.ds(0, 2)], am_recv.at[2])
    add_group(far, False)
    lext[...] = acc[...].astype(jnp.bfloat16)

    def b_copy(i):
        return remote(
            lext.at[pl.ds(pl.multiple_of(ROWS * i, ROWS), LROWS)],
            lbuf.at[w],
            b_send,
            b_recv.at[slot // 8],
            core_t,
            HALF * s + i,
            x,
        )

    def b_local():
        return pltpu.make_async_copy(
            lext.at[pl.ds(pl.multiple_of(ROWS * slot, ROWS), LROWS)], lbuf.at[w], b_recv.at[slot // 8]
        )

    @pl.loop(1, HALF)
    def _(step):
        b_copy((slot + step) % HALF).start()

    @pl.when(own_target)
    def _():
        b_local().start()

    @pl.when(jnp.logical_not(own_target))
    def _():
        b_copy(slot).start()

    c_arrive(2)
    c_arrive(3)

    mine = HALF * s
    theirs = HALF * (1 - s)

    def mirror(buf, first, count, send, recv):
        part = buf.at[pl.ds(first, count)]
        return remote(part, part, send, recv, *sister)

    for part in range(4):
        drain(lbuf.at[pl.ds(0, 8)], b_recv.at[part])
        mirror(lbuf, mine + 8 * part, 8, bm_send, bm_recv.at[part]).start()
        l32[pl.ds(mine + 8 * part, 8)] = lbuf[pl.ds(mine + 8 * part, 8)].astype(jnp.float32)
    c_arrive(4)
    for part in range(4):
        drain(lbuf.at[pl.ds(0, 8)], bm_recv.at[part])
        l32[pl.ds(theirs + 8 * part, 8)] = lbuf[pl.ds(theirs + 8 * part, 8)].astype(jnp.float32)
    drain(cmir.at[pl.ds(0, HALF)], cm_recv)

    def moved(series, i, start, rows):
        a = series[sources[i, s], pl.ds(start - delays[i, s], rows), :]
        b = series[sources[i, 1 - s], pl.ds(start - delays[i, 1 - s], rows), :]
        lhs = jnp.concatenate([a, b], axis=1).astype(jnp.bfloat16)
        turned = (i % RING) * RING + i // RING
        rhs = jnp.concatenate(
            [cown[jnp.where(first_core, i, turned)], cmir[jnp.where(first_core, turned, i)]], axis=0
        )
        return jnp.dot(lhs, rhs, preferred_element_type=jnp.float32)

    for part in range(4):

        @pl.loop(0, 8, unroll=4)
        def _(m):
            i = mine + 8 * part + m
            total = l32[i, HALO:LROWS, :] + moved(l32, i, HALO, FROWS)
            rounded = total.astype(jnp.bfloat16)
            fbuf[i] = rounded
            f32b[i] = rounded.astype(jnp.float32)

        mirror(fbuf, mine + 8 * part, 8, f_send, f_recv.at[part]).start()

    for part in range(4):
        drain(fbuf.at[pl.ds(0, 8)], f_recv.at[part])
        f32b[pl.ds(theirs + 8 * part, 8)] = fbuf[pl.ds(theirs + 8 * part, 8)].astype(jnp.float32)

    span = pl.ds(pl.multiple_of(ROWS * slot, ROWS), ROWS)

    def second(m):
        i = mine + m
        total = f32b[i, HALO:FROWS, :] + moved(f32b, i, HALO, ROWS)
        sbuf[m] = total.astype(jnp.bfloat16)

    def e_copy(m):
        return remote(sbuf.at[m], out.at[span], e_send, e_recv, core_t, mine + m, x)

    def e_local():
        return pltpu.make_async_copy(sbuf.at[slot], out.at[span], e_recv)

    second(slot)

    @pl.when(own_target)
    def _():
        e_local().start()

    @pl.when(jnp.logical_not(own_target))
    def _():
        e_copy(slot).start()

    @pl.loop(1, HALF)
    def _(step):
        m = (slot + step) % HALF
        second(m)
        e_copy(m).start()

    drain(out, e_recv)
    for copy in a_copies + [fwd_right, fwd_left]:
        copy.wait_send()
    drain(rbuf.at[pl.ds(0, 6)], am_send)
    drain(cown.at[pl.ds(0, RING - 1)], c1_send)
    drain(cown.at[pl.ds(0, 56)], c2_send)
    drain(cmir.at[pl.ds(0, HALF)], cm_send)
    drain(lbuf.at[pl.ds(0, HALF - 1)], b_send)
    drain(sbuf.at[pl.ds(0, HALF - 1)], e_send)

    @pl.when(jnp.logical_not(own_target))
    def _():
        drain(lbuf.at[0], b_send)
        drain(sbuf.at[0], e_send)

    drain(lbuf.at[pl.ds(0, HALF)], bm_send)
    drain(fbuf.at[pl.ds(0, HALF)], f_send)


def body(weather, response, coupling, sources, delays):
    pieces = response.reshape(BS, 4, PIECE * CH).transpose(1, 0, 2)
    bf16, f32 = jnp.bfloat16, jnp.float32
    vm, dma = pltpu.VMEM, pltpu.SemaphoreType.DMA
    rows = pl.pallas_call(
        kernel,
        out_shape=jax.ShapeDtypeStruct((QUARTER, BS), bf16),
        in_specs=[pl.BlockSpec(memory_space=pl.ANY)] * 3
        + [pl.BlockSpec(memory_space=pltpu.SMEM)] * 2,
        out_specs=pl.BlockSpec(memory_space=pl.ANY),
        scratch_shapes=[
            vm((WPRE + QUARTER, CH), bf16),
            vm((WPRE + QUARTER, CH), f32),
            vm((XROWS, GROUP * CH), bf16),
            vm((16, BS, PIECE * CH), bf16),
            vm((EXT, BS), f32),
            vm((EXT, BS), bf16),
            vm((BLOCKS, LROWS, BS), bf16),
            vm((BLOCKS, LROWS, BS), f32),
            vm((BLOCKS, FROWS, BS), bf16),
            vm((BLOCKS, FROWS, BS), f32),
            vm((HALF, ROWS, BS), bf16),
            vm((BLOCKS, BS, BS), bf16),
            vm((BLOCKS, BS, BS), bf16),
            dma((2,)),
            dma((2,)),
            dma,
            dma((6,)),
            dma((6,)),
            dma,
            dma((3,)),
            dma,
            dma,
            dma,
            dma((16,)),
            dma,
            dma,
            dma,
            dma((4,)),
            dma,
            dma((4,)),
            dma,
            dma((4,)),
            dma,
            dma,
        ],
        compiler_params=pltpu.CompilerParams(
            collective_id=0, has_side_effects=True, vmem_limit_bytes=40 * 1024 * 1024
        ),
    )(weather, pieces, coupling, sources, delays)
    return rows.T


def solution(mesh):
    placed = (P("scen", None), P("wide", "blk", None), P("wide", None, None, None), P(), P())
    return jax.shard_map(
        body, mesh=mesh, in_specs=placed, out_specs=P(("scen", "wide"), "blk"), check_vma=False
    )
```

time: 195 us -> 75.9 us (0.39)
  the two profiles are of different devices: /device:TPU:6 before, /device:TPU:5 now
where the time goes in v1:
time: 75.9 us; the launch traced here: 75.7 us
  Pallas kernels  72.2 us (95%)
  local copies, waits for them, and re-layouts  3.45 us (5%)
    pallas_call x1, Pallas kernels, body(): pl.pallas_call(kernel, out_shape=jax.ShapeDtypeStruct((QUARTER, BS), bf16...  72.2 us
    unnamed x11, local copies, waits for them, and re-layouts  2.39 us

profile of v1, /device:TPU:5, one launch (start us, length us, event | category | flops | bytes accessed | tf_op | source)
XLA Modules:
  0.0 75.7 jit_solution(13012840997191333032)
XLA Ops:
  0.0 0.0 copy-start
  0.0 1.5 %copy.9 = bf16[128,16,128]{0,2,1:T(8,128)(2,1)S(1)} copy(bf16[128,16,128]{2,1,0:T(8,128)(2,1)} %param.6) | data formatting | bytes 1048576 | tf_op args[1]
  1.6 0.0 copy-start.2
  1.6 0.0 copy-start.3
  1.6 0.2 copy.10
  1.8 0.0 copy-start.1
  1.8 0.4 copy-done.2
  2.2 0.1 copy.11.sources
  2.3 0.0 copy-done.3
  2.3 0.1 copy.12.delays
  2.4 0.0 copy-done
  2.4 0.2 copy-done.1
  2.6 72.2 %shard_map.55 = bf16[1024,128]{1,0:T(8,128)(2,1)S(1)} custom-call(bf16[4096,128]{1,0:T(8,128)(2,1)S(1)} %copy-done, bf16[4,128,512]{2,1,0:T(8,128)(2,1)S(1)} %bitcast.3, bf16[1,2,128,128]{3,2,1,0:T(8,128)(2,1)S(1)} %copy-done.1, s32[64,2]{1,0:T(8,128)S(1)} %copy.11.sources, s32[64,2]{1,0:T(8,128)S(1)} %copy.12.delays), custom_call_target="tpu_custom_call" | custom-call | tf_op jit(solution)/shard_map/pallas_call | solution.py:422
  74.9 0.9 %copy.13 = bf16[128,1024]{1,0:T(8,128)(2,1)} copy(bf16[128,1024]{0,1:T(8,128)(2,1)S(1)} %bitcast.4) | data formatting | bytes 524288 | tf_op jit(solution)/shard_map/transpose | solution.py:468
Async XLA Ops:
  0.0 2.4 %copy-start = (bf16[4096,128]{1,0:T(8,128)(2,1)S(1)}, bf16[4096,128]{1,0:T(8,128)(2,1)}, u32[]{:S(2)}) copy-start(bf16[4096,128]{1,0:T(8,128)(2,1)} %weather.1) | copy-start | bytes 3145732
  1.6 0.7 copy-start.2
  1.6 0.8 %copy-start.3 = (s32[64,2]{0,1:T(2,128)S(1)}, s32[64,2]{0,1:T(2,128)}, u32[]{:S(2)}) copy-start(s32[64,2]{0,1:T(2,128)} %param.9) | copy-start | bytes 1540
  1.8 0.8 %copy-start.1 = (bf16[1,2,128,128]{3,2,1,0:T(8,128)(2,1)S(1)}, bf16[1,2,128,128]{3,2,1,0:T(8,128)(2,1)}, u32[]{:S(2)}) copy-start(bf16[1,2,128,128]{3,2,1,0:T(8,128)(2,1)} %coupling.1) | copy-start | bytes 196612

commit v2 on v1

v2 whole, which is shorter than its diff:
```python
import functools

import jax
import jax.numpy as jnp
from jax import lax
from jax.experimental import pallas as pl
from jax.experimental.pallas import tpu as pltpu
from jax.sharding import PartitionSpec as P

MESH = pl.DeviceIdType.MESH
CH = 128
LAGS = 64
BS = 128
HALO = 16
RING = 8
BLOCKS = 64
HALF = 32
ROWS = 32
QUARTER = HALF * ROWS
EXT = QUARTER + 2 * HALO
LROWS = ROWS + 2 * HALO
FROWS = ROWS + HALO
PIECE = 4
PARTS = 4
GROUP = 16
XROWS = EXT + LAGS - GROUP
WPRE = 96
TILE = 352
STRIDE = 5


def drain(ref, sem):
    pltpu.make_async_copy(ref, ref, sem).wait()


def kernel(
    weather,
    resp,
    coupling,
    sources,
    delays,
    out,
    rraw,
    r32,
    wraw,
    w32,
    xbuf,
    rbuf,
    acc,
    lext,
    lbuf,
    l32,
    fbuf,
    f32b,
    sbuf,
    cown,
    loc_sem,
    own_sem,
    a_send,
    a_recv,
    am_send,
    am_recv,
    c1_send,
    c1_recv,
    c2_send,
    c2_recv,
    b_send,
    b_recv,
    bm_send,
    bm_recv,
    f_send,
    f_recv,
    e_send,
    e_recv,
):
    s = lax.axis_index("scen")
    w = lax.axis_index("wide")
    x = lax.axis_index("blk")
    y, z = w // RING, w % RING
    first_core = s == 0
    u = jnp.where(first_core, z, y)
    v = jnp.where(first_core, y, z)
    right, left = (x + 1) % PARTS, (x + PARTS - 1) % PARTS
    far = (x + 2) % PARTS

    def wide_of(uu, vv):
        return jnp.where(first_core, vv * RING + uu, uu * RING + vv)

    def remote(src, dst, send, recv, core, wide, blk):
        return pltpu.make_async_remote_copy(
            src_ref=src,
            dst_ref=dst,
            send_sem=send,
            recv_sem=recv,
            device_id=(core, wide, blk),
            device_id_type=MESH,
        )

    sister = (1 - s, w, x)
    core_t = (y + z) % 2
    slot = w // 2

    def chip(core, m):
        return 2 * m + (core + m // 4) % 2

    own_target = core_t == s

    lead = pl.multiple_of(jnp.maximum(x * QUARTER - WPRE, 0), 32)
    here = pl.multiple_of(x * QUARTER, QUARTER)
    main_copy = pltpu.make_async_copy(
        weather.at[pl.ds(here, QUARTER)], wraw.at[pl.ds(WPRE, QUARTER)], loc_sem.at[0]
    )
    lead_copy = pltpu.make_async_copy(
        weather.at[pl.ds(lead, WPRE)], wraw.at[pl.ds(0, WPRE)], loc_sem.at[1]
    )
    resp_copy = pltpu.make_async_copy(resp, rraw, own_sem)
    resp_copy.start()
    main_copy.start()
    lead_copy.start()

    barrier = pltpu.get_barrier_semaphore()

    def greet(core, wide, blk):
        pl.semaphore_signal(barrier, inc=1, device_id=(core, wide, blk), device_id_type=MESH)

    greet(s, w, right)
    greet(s, w, left)
    greet(*sister)

    @pl.loop(1, RING)
    def _(step):
        greet(s, wide_of((u + step) % RING, v), x)

    greet(s, wide_of(u, (v + 1) % RING), x)
    greet(s, wide_of(u, (v + RING - 1) % RING), x)

    @pl.loop(1, HALF)
    def _(step):
        greet(core_t, chip(s, (slot + step) % HALF), x)

    @pl.when(jnp.logical_not(own_target))
    def _():
        greet(core_t, chip(s, slot), x)

    def lay_out(core):
        for lag in range(GROUP // 2):
            column = (lag % PIECE) * CH
            rbuf[4 * x + 2 * core + lag // PIECE, :, column : column + CH] = r32[
                pl.ds(GROUP // 2 * core + lag, BS, stride=GROUP), :
            ].astype(jnp.bfloat16)

    resp_copy.wait()
    r32[...] = rraw[...].astype(jnp.float32)
    lay_out(s)

    pl.semaphore_wait(barrier, 3 + RING - 1 + 2 + HALF - 1 + jnp.where(own_target, 0, 1))

    def a_copy(index, src, piece, blk):
        return remote(src, rbuf.at[piece], a_send.at[index], a_recv.at[index], s, w, blk)

    p0, p1 = 2 * s, 2 * s + 1
    a_copies = [
        a_copy(0, rbuf.at[4 * x + p0], 4 * x + p0, right),
        a_copy(1, rbuf.at[4 * x + p1], 4 * x + p1, left),
        a_copy(2, rbuf.at[4 * x + p1], 4 * x + p1, right),
        a_copy(3, rbuf.at[4 * x + p0], 4 * x + p0, left),
    ]
    for copy in a_copies:
        copy.start()

    @pl.when(own_target)
    def _():
        pltpu.make_async_copy(coupling.at[0], cown.at[4 * v], c1_recv.at[0]).start()
        for away, place in ((1, 1), (7, 0), (2, 2), (6, 1), (3, 3), (5, 2), (4, 3)):
            remote(
                coupling.at[0],
                cown.at[4 * v + place],
                c1_send,
                c1_recv.at[place],
                s,
                wide_of((u + away) % RING, v),
                x,
            ).start()

    def c_step(way, step, piece):
        if way == 0:
            row, to = (v + RING - step + 1) % RING, (v + 1) % RING
        else:
            row, to = (v + step - 1) % RING, (v + RING - 1) % RING
        part = cown.at[4 * row + piece]
        index = (way * 4 + step - 1) * 4 + piece
        return remote(part, part, c2_send, c2_recv.at[index], s, wide_of(u, to), x)

    def goes(way, step, piece):
        return step < 4 or (step == 4 and piece // 2 == way)

    def c_begin(*pieces):
        for piece in pieces:
            drain(cown.at[0], c1_recv.at[piece])
            for way in range(2):
                c_step(way, 1, piece).start()

    def c_arrive(step, *pieces):
        for piece in pieces:
            for way in range(2):
                if goes(way, step, piece):
                    c_step(way, step, piece).wait_recv()
                    if goes(way, step + 1, piece):
                        c_step(way, step + 1, piece).start()

    main_copy.wait()
    lead_copy.wait()

    @pl.when(x == 0)
    def _():
        wraw[pl.ds(0, WPRE), :] = jnp.zeros((WPRE, CH), jnp.bfloat16)

    w32[...] = wraw[...].astype(jnp.float32)
    for lag in range(GROUP):
        xbuf[:, lag * CH : (lag + 1) * CH] = w32[GROUP - lag : GROUP - lag + XROWS, :].astype(
            jnp.bfloat16
        )

    def add_groups(groups, tile, first=False):
        total = None if first else acc[pl.ds(tile * TILE, TILE), :]
        for group in groups:
            start = pl.multiple_of((LAGS - GROUP) - GROUP * group + tile * TILE, 16)
            for piece in range(4):
                term = lax.dot_general(
                    xbuf[pl.ds(start, TILE), piece * PIECE * CH : (piece + 1) * PIECE * CH],
                    rbuf[4 * group + piece],
                    (((1,), (1,)), ((), ())),
                    preferred_element_type=jnp.float32,
                )
                total = term if total is None else total + term
        return total

    def keep(tile, total):
        acc[pl.ds(tile * TILE, TILE), :] = total

    lay_out(1 - s)
    c_begin(0)
    for tile in range(3):
        keep(tile, add_groups([x], tile, True))

    def mirror_piece(piece, group_sem):
        remote(
            rbuf.at[piece], rbuf.at[piece], am_send, am_recv.at[group_sem], *sister
        ).start()

    a_copies[0].wait_recv()
    fwd_right = a_copy(4, rbuf.at[4 * left + p0], 4 * left + p0, right)
    fwd_right.start()
    a_copies[1].wait_recv()
    fwd_left = a_copy(5, rbuf.at[4 * right + p1], 4 * right + p1, left)
    fwd_left.start()
    mirror_piece(4 * left + p0, 0)
    mirror_piece(4 * right + p1, 1)

    c_begin(1, 2, 3)

    c_arrive(1, 0)
    a_copies[2].wait_recv()
    mirror_piece(4 * left + p1, 0)
    a_copies[3].wait_recv()
    mirror_piece(4 * right + p0, 1)
    c_arrive(1, 1, 2)
    drain(rbuf.at[pl.ds(0, 2)], am_recv.at[0])
    drain(rbuf.at[pl.ds(0, 2)], am_recv.at[1])
    keep(0, add_groups([left, right], 0))
    c_arrive(1, 3)
    keep(1, add_groups([left, right], 1))
    c_arrive(2, 0)
    fwd_right.wait_recv()
    mirror_piece(4 * far + p0, 2)
    fwd_left.wait_recv()
    mirror_piece(4 * far + p1, 2)
    keep(2, add_groups([left, right], 2))
    c_arrive(2, 1, 2)
    drain(rbuf.at[pl.ds(0, 2)], am_recv.at[2])
    for tile in range(3):
        lext[pl.ds(tile * TILE, TILE), :] = add_groups([far], tile).astype(jnp.bfloat16)

    def b_copy(i):
        return remote(
            lext.at[pl.ds(pl.multiple_of(ROWS * i, ROWS), LROWS)],
            lbuf.at[HALF * core_t + slot],
            b_send,
            b_recv.at[slot // 8],
            core_t,
            chip(s, i),
            x,
        )

    def b_local():
        return pltpu.make_async_copy(
            lext.at[pl.ds(pl.multiple_of(ROWS * slot, ROWS), LROWS)], lbuf.at[HALF * core_t + slot], b_recv.at[slot // 8]
        )

    @pl.loop(1, HALF)
    def _(step):
        b_copy((slot + STRIDE * step) % HALF).start()

    @pl.when(own_target)
    def _():
        b_local().start()

    @pl.when(jnp.logical_not(own_target))
    def _():
        b_copy(slot).start()

    c_arrive(2, 3)
    c_arrive(3, 0, 1, 2, 3)
    c_arrive(4, 0, 2, 1, 3)

    mine = HALF * s
    theirs = HALF * (1 - s)

    def mirror(buf, first, count, send, recv):
        part = buf.at[pl.ds(first, count)]
        return remote(part, part, send, recv, *sister)

    for part in range(4):
        drain(lbuf.at[pl.ds(0, 8)], b_recv.at[part])
        mirror(lbuf, mine + 8 * part, 8, bm_send, bm_recv.at[part]).start()
        l32[pl.ds(mine + 8 * part, 8)] = lbuf[pl.ds(mine + 8 * part, 8)].astype(jnp.float32)
    for part in range(4):
        drain(lbuf.at[pl.ds(0, 8)], bm_recv.at[part])
        l32[pl.ds(theirs + 8 * part, 8)] = lbuf[pl.ds(theirs + 8 * part, 8)].astype(jnp.float32)

    def block_of(wide):
        return HALF * ((wide // RING + wide) % 2) + wide // 2

    def moved(series, m, start, rows):
        wide = chip(s, m)
        upstream = [
            series[block_of(sources[k, wide]), pl.ds(start - delays[k, wide], rows), :]
            for k in range(2)
        ]
        lhs = jnp.concatenate(upstream, axis=1).astype(jnp.bfloat16)
        wy, wz = wide // RING, wide % RING
        row = jnp.where(first_core, wy, wz)
        away = (jnp.where(first_core, wz, wy) - u + RING) % RING
        place = jnp.where(
            away % 2 == 0,
            jnp.where(away == 0, 0, jnp.where(away == 2, 1, jnp.where(away == 6, 2, 3))),
            jnp.where(away == 1, 0, jnp.where(away == 7, 1, jnp.where(away == 3, 2, 3))),
        )
        rhs = cown[4 * row + place].reshape(2 * BS, BS)
        return jnp.dot(lhs, rhs, preferred_element_type=jnp.float32)

    for part in range(4):

        @pl.loop(0, 8, unroll=8)
        def _(m):
            i = mine + 8 * part + m
            total = l32[i, HALO:LROWS, :] + moved(l32, 8 * part + m, HALO, FROWS)
            rounded = total.astype(jnp.bfloat16)
            fbuf[i] = rounded
            f32b[i] = rounded.astype(jnp.float32)

        mirror(fbuf, mine + 8 * part, 8, f_send, f_recv.at[part]).start()

    for part in range(4):
        drain(fbuf.at[pl.ds(0, 8)], f_recv.at[part])
        f32b[pl.ds(theirs + 8 * part, 8)] = fbuf[pl.ds(theirs + 8 * part, 8)].astype(jnp.float32)

    span = pl.ds(pl.multiple_of(ROWS * slot, ROWS), ROWS)

    def second(m):
        i = mine + m
        total = f32b[i, HALO:FROWS, :] + moved(f32b, m, HALO, ROWS)
        sbuf[m] = total.astype(jnp.bfloat16)

    def e_copy(m):
        return remote(sbuf.at[m], out.at[span], e_send, e_recv, core_t, chip(s, m), x)

    def e_local():
        return pltpu.make_async_copy(sbuf.at[slot], out.at[span], e_recv)

    second(slot)

    @pl.when(own_target)
    def _():
        e_local().start()

    @pl.when(jnp.logical_not(own_target))
    def _():
        e_copy(slot).start()

    def second_batch(first, count):
        picked = [(slot + first + k) % HALF for k in range(count)]
        for m in picked:
            second(m)
        for m in picked:
            e_copy(m).start()

    second_batch(1, 3)

    @pl.loop(1, 8)
    def _(batch):
        second_batch(4 * batch, 4)

    drain(out, e_recv)
    for copy in a_copies + [fwd_right, fwd_left]:
        copy.wait_send()
    drain(rbuf.at[pl.ds(0, 6)], am_send)
    drain(cown.at[pl.ds(0, 28)], c2_send)

    @pl.when(own_target)
    def _():
        drain(cown.at[pl.ds(0, RING - 1)], c1_send)

    drain(lbuf.at[pl.ds(0, HALF - 1)], b_send)
    drain(sbuf.at[pl.ds(0, HALF - 1)], e_send)

    @pl.when(jnp.logical_not(own_target))
    def _():
        drain(lbuf.at[0], b_send)
        drain(sbuf.at[0], e_send)

    drain(lbuf.at[pl.ds(0, HALF)], bm_send)
    drain(fbuf.at[pl.ds(0, HALF)], f_send)


def body(weather, response, coupling, sources, delays):
    rows_of_lags = response.reshape(BS * GROUP, CH)
    bf16, f32 = jnp.bfloat16, jnp.float32
    vm, dma = pltpu.VMEM, pltpu.SemaphoreType.DMA
    rows = pl.pallas_call(
        kernel,
        out_shape=jax.ShapeDtypeStruct((QUARTER, BS), bf16),
        in_specs=[pl.BlockSpec(memory_space=pltpu.HBM)] * 3
        + [pl.BlockSpec(memory_space=pltpu.SMEM)] * 2,
        out_specs=pl.BlockSpec(memory_space=pl.ANY),
        scratch_shapes=[
            vm((BS * GROUP, CH), bf16),
            vm((BS * GROUP, CH), f32),
            vm((WPRE + QUARTER, CH), bf16),
            vm((WPRE + QUARTER, CH), f32),
            vm((XROWS, GROUP * CH), bf16),
            vm((16, BS, PIECE * CH), bf16),
            vm((EXT, BS), f32),
            vm((EXT, BS), bf16),
            vm((BLOCKS, LROWS, BS), bf16),
            vm((BLOCKS, LROWS, BS), f32),
            vm((BLOCKS, FROWS, BS), bf16),
            vm((BLOCKS, FROWS, BS), f32),
            vm((HALF, ROWS, BS), bf16),
            vm((HALF, 2, BS, BS), bf16),
            dma((2,)),
            dma,
            dma((6,)),
            dma((6,)),
            dma,
            dma((3,)),
            dma,
            dma((4,)),
            dma,
            dma((32,)),
            dma,
            dma((4,)),
            dma,
            dma((4,)),
            dma,
            dma((4,)),
            dma,
            dma,
        ],
        compiler_params=pltpu.CompilerParams(
            collective_id=0, has_side_effects=True, vmem_limit_bytes=60 * 1024 * 1024
        ),
    )(weather, rows_of_lags, coupling, sources.T, delays.T)
    return rows.T


def solution(mesh):
    placed = (P("scen", None), P("wide", "blk", None), P("wide", None, None, None), P(), P())
    return jax.shard_map(
        body, mesh=mesh, in_specs=placed, out_specs=P(("scen", "wide"), "blk"), check_vma=False
    )
```

time: 75.9 us -> 70.3 us (0.926)
  the two profiles are of different devices: /device:TPU:5 before, /device:TPU:6 now
where the time goes in v2:
time: 70.3 us; the launch traced here: 69.4 us
  Pallas kernels  67.6 us (96%)
  local copies, waits for them, and re-layouts  1.79 us (3%)
    pallas_call x1, Pallas kernels, body(): pl.pallas_call(kernel, out_shape=jax.ShapeDtypeStruct((QUARTER, BS), bf16...  67.6 us
    transpose x1, local copies, waits for them, and re-layouts, body(): return rows.T  1.79 us

profile of v2, /device:TPU:6, one launch (start us, length us, event | category | flops | bytes accessed | tf_op | source)
XLA Modules:
  0.0 69.4 jit_solution(16551056858068027701)
XLA Ops:
  0.0 67.6 %shard_map.55 = bf16[1024,128]{1,0:T(8,128)(2,1)} custom-call(bf16[4096,128]{1,0:T(8,128)(2,1)} %weather.1, bf16[2048,128]{1,0:T(8,128)(2,1)} %bitcast.5, bf16[1,2,128,128]{3,2,1,0:T(8,128)(2,1)} %coupling.1, s32[2,64]{1,0:T(2,128)} %bitcast.6, s32[2,64]{1,0:T(2,128)} %bitcast.7), custom_call_target="tpu_custom_call" | custom-call | tf_op jit(solution)/shard_map/pallas_call | solution.py:430
  67.6 1.8 %copy.6 = bf16[128,1024]{1,0:T(8,128)(2,1)} copy(bf16[128,1024]{0,1:T(8,128)(2,1)} %bitcast.4) | data formatting | bytes 524288 | tf_op jit(solution)/shard_map/transpose | solution.py:474

commit v3 on v2

--- a/solution.py
+++ b/solution.py
@@ -216,10 +216,17 @@
         wraw[pl.ds(0, WPRE), :] = jnp.zeros((WPRE, CH), jnp.bfloat16)
 
     w32[...] = wraw[...].astype(jnp.float32)
-    for lag in range(GROUP):
-        xbuf[:, lag * CH : (lag + 1) * CH] = w32[GROUP - lag : GROUP - lag + XROWS, :].astype(
-            jnp.bfloat16
-        )
+
+    def columns(first, last):
+        for lag in range(first, last):
+            xbuf[:, lag * CH : (lag + 1) * CH] = w32[GROUP - lag : GROUP - lag + XROWS, :].astype(
+                jnp.bfloat16
+            )
+
+    columns(0, 8)
+    c_begin(0)
+    columns(8, 16)
+    c_begin(1)
 
     def add_groups(groups, tile, first=False):
         total = None if first else acc[pl.ds(tile * TILE, TILE), :]
@@ -235,13 +242,26 @@
                 total = term if total is None else total + term
         return total
 
+    def add_far(core, tile):
+        start = pl.multiple_of((LAGS - GROUP) - GROUP * far + tile * TILE, 16)
+        total = acc[pl.ds(tile * TILE, TILE), :]
+        for half in range(2):
+            piece = 2 * core + half
+            column = pl.multiple_of(piece * PIECE * CH, PIECE * CH)
+            total = total + lax.dot_general(
+                xbuf[pl.ds(start, TILE), pl.ds(column, PIECE * CH)],
+                rbuf[4 * far + piece],
+                (((1,), (1,)), ((), ())),
+                preferred_element_type=jnp.float32,
+            )
+        return total
+
     def keep(tile, total):
         acc[pl.ds(tile * TILE, TILE), :] = total
 
     lay_out(1 - s)
-    c_begin(0)
-    for tile in range(3):
-        keep(tile, add_groups([x], tile, True))
+    keep(0, add_groups([x], 0, True))
+    keep(1, add_groups([x], 1, True))
 
     def mirror_piece(piece, group_sem):
         remote(
@@ -257,31 +277,37 @@
     mirror_piece(4 * left + p0, 0)
     mirror_piece(4 * right + p1, 1)
 
-    c_begin(1, 2, 3)
-
+    c_begin(2)
     c_arrive(1, 0)
+    keep(2, add_groups([x], 2, True))
+    c_begin(3)
+    c_arrive(1, 1)
     a_copies[2].wait_recv()
     mirror_piece(4 * left + p1, 0)
     a_copies[3].wait_recv()
     mirror_piece(4 * right + p0, 1)
-    c_arrive(1, 1, 2)
+    c_arrive(1, 2, 3)
+    c_arrive(2, 0)
     drain(rbuf.at[pl.ds(0, 2)], am_recv.at[0])
     drain(rbuf.at[pl.ds(0, 2)], am_recv.at[1])
     keep(0, add_groups([left, right], 0))
-    c_arrive(1, 3)
+    c_arrive(2, 1)
     keep(1, add_groups([left, right], 1))
-    c_arrive(2, 0)
+    c_arrive(2, 2)
     fwd_right.wait_recv()
     mirror_piece(4 * far + p0, 2)
     fwd_left.wait_recv()
     mirror_piece(4 * far + p1, 2)
     keep(2, add_groups([left, right], 2))
-    c_arrive(2, 1, 2)
+    for tile in range(3):
+        keep(tile, add_far(s, tile))
+    c_arrive(2, 3)
     drain(rbuf.at[pl.ds(0, 2)], am_recv.at[2])
     for tile in range(3):
-        lext[pl.ds(tile * TILE, TILE), :] = add_groups([far], tile).astype(jnp.bfloat16)
-
-    def b_copy(i):
+        lext[pl.ds(tile * TILE, TILE), :] = add_far(1 - s, tile).astype(jnp.bfloat16)
+
+    def b_copy(step):
+        i = (slot + STRIDE * step) % HALF
         return remote(
             lext.at[pl.ds(pl.multiple_of(ROWS * i, ROWS), LROWS)],
             lbuf.at[HALF * core_t + slot],
@@ -292,24 +318,22 @@
             x,
         )
 
-    def b_local():
-        return pltpu.make_async_copy(
-            lext.at[pl.ds(pl.multiple_of(ROWS * slot, ROWS), LROWS)], lbuf.at[HALF * core_t + slot], b_recv.at[slot // 8]
-        )
+    @pl.when(own_target)
+    def _():
+        pltpu.make_async_copy(
+            lext.at[pl.ds(pl.multiple_of(ROWS * slot, ROWS), LROWS)],
+            lbuf.at[HALF * core_t + slot],
+            b_recv.at[slot // 8],
+        ).start()
+
+    @pl.when(jnp.logical_not(own_target))
+    def _():
+        b_copy(0).start()
 
     @pl.loop(1, HALF)
     def _(step):
-        b_copy((slot + STRIDE * step) % HALF).start()
-
-    @pl.when(own_target)
-    def _():
-        b_local().start()
-
-    @pl.when(jnp.logical_not(own_target))
-    def _():
-        b_copy(slot).start()
-
-    c_arrive(2, 3)
+        b_copy(step).start()
+
     c_arrive(3, 0, 1, 2, 3)
     c_arrive(4, 0, 2, 1, 3)
 
@@ -320,13 +344,17 @@
         part = buf.at[pl.ds(first, count)]
         return remote(part, part, send, recv, *sister)
 
+    def widen(first):
+        l32[pl.ds(first, 8)] = lbuf[pl.ds(first, 8)].astype(jnp.float32)
+
     for part in range(4):
         drain(lbuf.at[pl.ds(0, 8)], b_recv.at[part])
         mirror(lbuf, mine + 8 * part, 8, bm_send, bm_recv.at[part]).start()
-        l32[pl.ds(mine + 8 * part, 8)] = lbuf[pl.ds(mine + 8 * part, 8)].astype(jnp.float32)
+    for part in range(4):
+        widen(mine + 8 * part)
     for part in range(4):
         drain(lbuf.at[pl.ds(0, 8)], bm_recv.at[part])
-        l32[pl.ds(theirs + 8 * part, 8)] = lbuf[pl.ds(theirs + 8 * part, 8)].astype(jnp.float32)
+        widen(theirs + 8 * part)
 
     def block_of(wide):
         return HALF * ((wide // RING + wide) % 2) + wide // 2
@@ -378,28 +406,25 @@
     def e_local():
         return pltpu.make_async_copy(sbuf.at[slot], out.at[span], e_recv)
 
-    second(slot)
-
-    @pl.when(own_target)
-    def _():
-        e_local().start()
-
-    @pl.when(jnp.logical_not(own_target))
-    def _():
-        e_copy(slot).start()
-
-    def second_batch(first, count):
-        picked = [(slot + first + k) % HALF for k in range(count)]
-        for m in picked:
-            second(m)
-        for m in picked:
-            e_copy(m).start()
-
-    second_batch(1, 3)
-
-    @pl.loop(1, 8)
-    def _(batch):
-        second_batch(4 * batch, 4)
+    @pl.loop(0, 4)
+    def _(column):
+        for start in (0, 4):
+            picked = [4 * ((y + start + k) % RING) + column for k in range(4)]
+            for m in picked:
+                second(m)
+            for k, m in enumerate(picked):
+                if start + k > 0:
+                    e_copy(m).start()
+                    continue
+                stays = jnp.logical_and(own_target, m == slot)
+
+                @pl.when(stays)
+                def _():
+                    e_local().start()
+
+                @pl.when(jnp.logical_not(stays))
+                def _():
+                    e_copy(m).start()
 
     drain(out, e_recv)
     for copy in a_copies + [fwd_right, fwd_left]:

time: 70.3 us -> 67 us (0.953)
  Pallas kernels: 67.6 us -> 65 us
    pallas_call x1, Pallas kernels: 67.6 us -> 65 us  [body(): pl.pallas_call(kernel, out_shape=jax.ShapeDtypeStruct((QUARTER, BS), bf16...]
where the time goes in v3:
time: 67 us; the launch traced here: 66.8 us
  Pallas kernels  65 us (97%)
  local copies, waits for them, and re-layouts  1.79 us (3%)
    pallas_call x1, Pallas kernels, body(): pl.pallas_call(kernel, out_shape=jax.ShapeDtypeStruct((QUARTER, BS), bf16...  65 us
    transpose x1, local copies, waits for them, and re-layouts, body(): return rows.T  1.79 us

profile of v3, /device:TPU:6, one launch (start us, length us, event | category | flops | bytes accessed | tf_op | source)
XLA Modules:
  0.0 66.8 jit_solution(14618275416131105055)
XLA Ops:
  0.0 65.0 %shard_map.55 = bf16[1024,128]{1,0:T(8,128)(2,1)} custom-call(bf16[4096,128]{1,0:T(8,128)(2,1)} %weather.1, bf16[2048,128]{1,0:T(8,128)(2,1)} %bitcast.5, bf16[1,2,128,128]{3,2,1,0:T(8,128)(2,1)} %coupling.1, s32[2,64]{1,0:T(2,128)} %bitcast.6, s32[2,64]{1,0:T(2,128)} %bitcast.7), custom_call_target="tpu_custom_call" | custom-call | tf_op jit(solution)/shard_map/pallas_call | solution.py:455
  65.0 1.8 %copy.6 = bf16[128,1024]{1,0:T(8,128)(2,1)} copy(bf16[128,1024]{0,1:T(8,128)(2,1)} %bitcast.4) | data formatting | bytes 524288 | tf_op jit(solution)/shard_map/transpose | solution.py:499

commit v4 on v3

--- a/solution.py
+++ b/solution.py
@@ -408,12 +408,12 @@
 
     @pl.loop(0, 4)
     def _(column):
-        for start in (0, 4):
-            picked = [4 * ((y + start + k) % RING) + column for k in range(4)]
+        for row in (s, 1 - s):
+            picked = [4 * (row + 2 * ((y // 2 + k) % 4)) + column for k in range(4)]
             for m in picked:
                 second(m)
             for k, m in enumerate(picked):
-                if start + k > 0:
+                if k > 0:
                     e_copy(m).start()
                     continue
                 stays = jnp.logical_and(own_target, m == slot)

time: 67 us -> 66.7 us (level)
  no operation moved by 1% of the time
where the time goes in v4:
time: 66.7 us; the launch traced here: 66.5 us
  Pallas kernels  64.7 us (97%)
  local copies, waits for them, and re-layouts  1.79 us (3%)
    pallas_call x1, Pallas kernels, body(): pl.pallas_call(kernel, out_shape=jax.ShapeDtypeStruct((QUARTER, BS), bf16...  64.7 us
    transpose x1, local copies, waits for them, and re-layouts, body(): return rows.T  1.79 us

profile of v4, /device:TPU:6, one launch (start us, length us, event | category | flops | bytes accessed | tf_op | source)
XLA Modules:
  0.0 66.5 jit_solution(9884871409581468047)
XLA Ops:
  0.0 64.7 %shard_map.55 = bf16[1024,128]{1,0:T(8,128)(2,1)} custom-call(bf16[4096,128]{1,0:T(8,128)(2,1)} %weather.1, bf16[2048,128]{1,0:T(8,128)(2,1)} %bitcast.5, bf16[1,2,128,128]{3,2,1,0:T(8,128)(2,1)} %coupling.1, s32[2,64]{1,0:T(2,128)} %bitcast.6, s32[2,64]{1,0:T(2,128)} %bitcast.7), custom_call_target="tpu_custom_call" | custom-call | tf_op jit(solution)/shard_map/pallas_call | solution.py:455
  64.7 1.8 %copy.6 = bf16[128,1024]{1,0:T(8,128)(2,1)} copy(bf16[128,1024]{0,1:T(8,128)(2,1)} %bitcast.4) | data formatting | bytes 524288 | tf_op jit(solution)/shard_map/transpose | solution.py:499

commit v5 on v4

--- a/solution.py
+++ b/solution.py
@@ -335,7 +335,6 @@
         b_copy(step).start()
 
     c_arrive(3, 0, 1, 2, 3)
-    c_arrive(4, 0, 2, 1, 3)
 
     mine = HALF * s
     theirs = HALF * (1 - s)
@@ -350,6 +349,7 @@
     for part in range(4):
         drain(lbuf.at[pl.ds(0, 8)], b_recv.at[part])
         mirror(lbuf, mine + 8 * part, 8, bm_send, bm_recv.at[part]).start()
+    c_arrive(4, 0, 2, 1, 3)
     for part in range(4):
         widen(mine + 8 * part)
     for part in range(4):

time: 66.7 us -> 66.7 us (level)
  no operation moved by 1% of the time
where the time goes in v5:
time: 66.7 us; the launch traced here: 66.4 us
  Pallas kernels  64.6 us (97%)
  local copies, waits for them, and re-layouts  1.79 us (3%)
    pallas_call x1, Pallas kernels, body(): pl.pallas_call(kernel, out_shape=jax.ShapeDtypeStruct((QUARTER, BS), bf16...  64.6 us
    transpose x1, local copies, waits for them, and re-layouts, body(): return rows.T  1.79 us

profile of v5, /device:TPU:6, one launch (start us, length us, event | category | flops | bytes accessed | tf_op | source)
XLA Modules:
  0.0 66.4 jit_solution(16908882957094577438)
XLA Ops:
  0.0 64.6 %shard_map.55 = bf16[1024,128]{1,0:T(8,128)(2,1)} custom-call(bf16[4096,128]{1,0:T(8,128)(2,1)} %weather.1, bf16[2048,128]{1,0:T(8,128)(2,1)} %bitcast.5, bf16[1,2,128,128]{3,2,1,0:T(8,128)(2,1)} %coupling.1, s32[2,64]{1,0:T(2,128)} %bitcast.6, s32[2,64]{1,0:T(2,128)} %bitcast.7), custom_call_target="tpu_custom_call" | custom-call | tf_op jit(solution)/shard_map/pallas_call | solution.py:455
  64.7 1.8 %copy.6 = bf16[128,1024]{1,0:T(8,128)(2,1)} copy(bf16[128,1024]{0,1:T(8,128)(2,1)} %bitcast.4) | data formatting | bytes 524288 | tf_op jit(solution)/shard_map/transpose | solution.py:499

commit v6 on v4

--- a/solution.py
+++ b/solution.py
@@ -410,9 +410,10 @@
     def _(column):
         for row in (s, 1 - s):
             picked = [4 * (row + 2 * ((y // 2 + k) % 4)) + column for k in range(4)]
-            for m in picked:
-                second(m)
             for k, m in enumerate(picked):
+                if k % 2 == 0:
+                    second(m)
+                    second(picked[k + 1])
                 if k > 0:
                     e_copy(m).start()
                     continue

time: 66.7 us -> 66.7 us (level)
  no operation moved by 1% of the time
where the time goes in v6:
time: 66.7 us; the launch traced here: 66.5 us
  Pallas kernels  64.7 us (97%)
  local copies, waits for them, and re-layouts  1.79 us (3%)
    pallas_call x1, Pallas kernels, body(): pl.pallas_call(kernel, out_shape=jax.ShapeDtypeStruct((QUARTER, BS), bf16...  64.7 us
    transpose x1, local copies, waits for them, and re-layouts, body(): return rows.T  1.79 us

profile of v6, /device:TPU:6, one launch (start us, length us, event | category | flops | bytes accessed | tf_op | source)
XLA Modules:
  0.0 66.5 jit_solution(5639067640272910574)
XLA Ops:
  0.0 64.7 %shard_map.55 = bf16[1024,128]{1,0:T(8,128)(2,1)} custom-call(bf16[4096,128]{1,0:T(8,128)(2,1)} %weather.1, bf16[2048,128]{1,0:T(8,128)(2,1)} %bitcast.5, bf16[1,2,128,128]{3,2,1,0:T(8,128)(2,1)} %coupling.1, s32[2,64]{1,0:T(2,128)} %bitcast.6, s32[2,64]{1,0:T(2,128)} %bitcast.7), custom_call_target="tpu_custom_call" | custom-call | tf_op jit(solution)/shard_map/pallas_call | solution.py:456
  64.7 1.8 %copy.6 = bf16[128,1024]{1,0:T(8,128)(2,1)} copy(bf16[128,1024]{0,1:T(8,128)(2,1)} %bitcast.4) | data formatting | bytes 524288 | tf_op jit(solution)/shard_map/transpose | solution.py:500
